TPU v7x, 256 devices: a whole 4x4x8 slice. The times are simulated.
256 devices in a mesh: blk: 32 (over y_lo, z, core), dp: 8 (over x, y_hi).
Axes of the slice: x: 4, y: 4 (y_hi: 2, y_lo: 2; y = y_hi * 2 + y_lo), z: 8, core: 2. Of those that a mesh axis runs over, the one named last changes fastest.
Arguments:
- residuals: bfloat16 [32768, 768], P(('blk', 'dp')), may hold values from -130 to 130
- codebook: bfloat16 [24576, 768], P('blk'), may hold values from -9 to 9
- section_codes: int32 [32768], P(('blk', 'dp')), may hold values from 0 to 1023, as said below
- code_owner: int32 [1024], replicated, may hold values from 0 to 31, as said below
Outputs:
- new_codebook: float32 [24576, 768], P('blk')
- code_shift: float32 [2048, 768], P('blk')
Inputs may be any that keep to these rules, and one draw needn't show every extreme that they name: `section_codes`: among the rows of one device, at most 12 have section-one codes owned by one codeword block, and in every device's rows some block is named exactly 12 times. `code_owner`: each codeword block owns at least one and at most 64 section-one codes; some block owns exactly 64.
All inputs are finite; a program needn't handle non-finite values.
Results may differ from a plain program's by a relative error of at most 0.002.
Values may be sent and summed in bfloat16 or wider, within the bound.
No kernel may reach another device: no remote copies, remote signals or barrier semaphores. Data moves between devices by JAX's collectives and lax.ppermute only.
A program may use at most 128 MiB of HBM per device.

v0:
```python
import math
import jax
import jax.numpy as jnp
from jax import lax
from jax.sharding import PartitionSpec as P

SLOTS = 64
prior_weight = 0.5


def merged(value, axis, join):
    pieces = jax.tree.map(lambda part: lax.all_gather(part, axis), value)
    head = jax.tree.map(lambda part: part[0], pieces)
    tail = jax.tree.map(lambda part: part[1:], pieces)
    running, _ = lax.scan(lambda running, section: (join(running, section), None), head, tail)
    return running


def score_block(rows, codebook, half_norm):
    raw = lax.dot_general(
        rows, codebook, (((1,), (1,)), ((), ())), preferred_element_type=jnp.float32
    )
    return (raw - half_norm[None, :]) * (2.0 / math.sqrt(rows.shape[1]))


def block_rows():
    return 512


def row_stats(rows, codebook, half_norm):
    count = rows.shape[0]
    size = block_rows()
    stacked = rows.reshape(count // size, size, rows.shape[1])

    def one_block(block):
        scores = score_block(block, codebook, half_norm)
        top = jnp.max(scores, axis=1)
        total = jnp.sum(jnp.exp(scores - top[:, None]), axis=1)
        return (top, total)

    top, total = lax.map(one_block, stacked)
    return (top.reshape(-1), total.reshape(-1))


def accumulate(carry, rows, top, total, codebook, half_norm):
    count = rows.shape[0]
    size = block_rows()
    stacked = rows.reshape(count // size, size, rows.shape[1])
    tops = top.reshape(count // size, size)
    totals = total.reshape(count // size, size)

    def add_weights(state, block, scores, block_top, block_total):
        weights = (jnp.exp(scores - block_top[:, None]) / block_total[:, None]).astype(jnp.bfloat16)
        weighted = state[0] + lax.dot_general(
            weights, block, (((0,), (0,)), ((), ())), preferred_element_type=jnp.float32
        )
        mass = state[1] + jnp.sum(weights.astype(jnp.float32), axis=0)
        return (weighted, mass)

    def fresh_block(state, item):
        block, block_top, block_total = item
        scores = score_block(block, codebook, half_norm)
        return (add_weights(state, block, scores, block_top, block_total), None)

    result, _ = lax.scan(fresh_block, carry, (stacked, tops, totals))
    return result


def combine_stats(first, second):
    top = jnp.maximum(first[0], second[0])
    total = first[1] * jnp.exp(first[0] - top) + second[1] * jnp.exp(second[0] - top)
    return (top, total)


def local(residuals, codebook, section_codes, code_owner):
    nblk = lax.axis_size("blk")
    row_count, width = residuals.shape
    half_norm = 0.5 * jnp.sum(jnp.square(codebook.astype(jnp.float32)), axis=1)
    top, total = row_stats(
        lax.all_gather(residuals, "blk", axis=0, tiled=True), codebook, half_norm
    )
    local_stats = (top, total)
    top_all, total_all = merged(local_stats, "blk", combine_stats)
    zero_sums = (
        jnp.zeros((codebook.shape[0], width), jnp.float32),
        jnp.zeros((codebook.shape[0],), jnp.float32),
    )
    top = top_all
    total = total_all
    weighted, mass = accumulate(
        zero_sums,
        lax.all_gather(residuals, "blk", axis=0, tiled=True),
        top,
        total,
        codebook,
        half_norm,
    )
    code_count = code_owner.shape[0]
    owner_hot = (code_owner[:, None] == jnp.arange(nblk, dtype=jnp.int32)[None, :]).astype(
        jnp.int32
    )
    before = jnp.cumsum(owner_hot, axis=0) - owner_hot
    rank = jnp.sum(before * owner_hot, axis=1)
    code_slot = code_owner * SLOTS + rank
    code_hit = section_codes[:, None] == jnp.arange(code_count, dtype=jnp.int32)[None, :]
    row_slot = jnp.sum(jnp.where(code_hit, code_slot[None, :], 0), axis=1)
    capacity = max(2, 3 * row_count // nblk)
    target = row_slot // SLOTS
    local_slot = row_slot - target * SLOTS
    target_hot = (target[:, None] == jnp.arange(nblk, dtype=jnp.int32)[None, :]).astype(jnp.int32)
    earlier = jnp.cumsum(target_hot, axis=0) - target_hot
    position = jnp.sum(earlier * target_hot, axis=1)
    flat_index = target * capacity + position
    row_buffer = jnp.zeros((nblk * capacity, width), jnp.bfloat16).at[flat_index].set(residuals)
    slot_hot = (local_slot[:, None] == jnp.arange(SLOTS, dtype=jnp.int32)[None, :]).astype(
        jnp.bfloat16
    )
    tag_buffer = jnp.zeros((nblk * capacity, SLOTS), jnp.bfloat16).at[flat_index].set(slot_hot)
    got_rows, got_tags = (
        lax.all_to_all(
            row_buffer.reshape(nblk, capacity, width),
            "blk",
            split_axis=0,
            concat_axis=0,
            tiled=True,
        ),
        lax.all_to_all(
            tag_buffer.reshape(nblk, capacity, SLOTS),
            "blk",
            split_axis=0,
            concat_axis=0,
            tiled=True,
        ),
    )
    tags_flat = got_tags.reshape(nblk * capacity, SLOTS)
    shift_sum = lax.dot_general(
        tags_flat,
        got_rows.reshape(nblk * capacity, width),
        (((0,), (0,)), ((), ())),
        preferred_element_type=jnp.float32,
    )
    shift_count = jnp.sum(tags_flat.astype(jnp.float32), axis=0)
    weighted, mass, shift_sum, shift_count = lax.psum(
        (weighted, mass, shift_sum, shift_count), "dp"
    )
    new_codebook = (weighted + prior_weight * codebook.astype(jnp.float32)) / (mass + prior_weight)[
        :, None
    ]
    code_shift = shift_sum / (shift_count + 1.0)[:, None]
    return (new_codebook, code_shift)


def solution(mesh):
    in_specs = (P(("blk", "dp"), None), P("blk", None), P(("blk", "dp")), P())
    out_specs = (P("blk", None), P("blk", None))
    return jax.shard_map(local, mesh=mesh, in_specs=in_specs, out_specs=out_specs, check_vma=False)
```

profile of v0, /device:TPU:50, one launch (start us, length us, event | category | flops | bytes accessed | tf_op | source)
XLA Modules:
  0.0 416.6 jit_solution(8335260162383934717)
XLA Ops:
  8.6 9.0 %reduce-window.6 = s32[32,8,128]{2,1,0:T(8,128)S(1)} reduce-window(s32[32,8,128]{2,1,0:T(8,128)S(1)} %fusion.18, s32[]{:T(128)} %constant.71.clone.1), window={size=1x1x128 pad=0_0x0_0x127_0}, to_apply=%region_12.13 | reduce-window | flops 4161536 | bytes 262148 | tf_op jit(solution)/shard_map/reduce-window
  22.6 9.4 %all-to-all-start = ((bf16[32,2,384]{2,1,0:T(2,128)(2,1)}), bf16[32,2,384]{2,1,0:T(2,128)(2,1)S(1)}, u32[]{:S(2)}, u32[]{:S(2)}) async-start(bf16[32,2,384]{2,1,0:T(2,128)(2,1)} %reshape.162), calls=%async_computation | async-start | bytes 98304 | tf_op jit(solution)/shard_map/all_to_all | solution.py:127
  34.8 5.1 %all-to-all-done = bf16[32,2,384]{2,1,0:T(2,128)(2,1)S(1)} async-done(((bf16[32,2,384]{2,1,0:T(2,128)(2,1)}), bf16[32,2,384]{2,1,0:T(2,128)(2,1)S(1)}, u32[]{:S(2)}, u32[]{:S(2)}) %all-to-all-start) | async-done | bytes 49184 | tf_op jit(solution)/shard_map/all_to_all | solution.py:127
  39.9 5.0 %all-to-all-start.1 = ((bf16[32,12,768]{2,1,0:T(8,128)(2,1)}), bf16[32,12,768]{2,1,0:T(8,128)(2,1)S(1)}, u32[]{:S(2)}, u32[]{:S(2)}) async-start(bf16[32,12,768]{2,1,0:T(8,128)(2,1)} %reshape.128), calls=%async_computation.1 | async-start | bytes 1572864 | tf_op jit(solution)/shard_map/all_to_all | solution.py:120
  46.8 30.1 %all-to-all-done.1 = bf16[32,12,768]{2,1,0:T(8,128)(2,1)S(1)} async-done(((bf16[32,12,768]{2,1,0:T(8,128)(2,1)}), bf16[32,12,768]{2,1,0:T(8,128)(2,1)S(1)}, u32[]{:S(2)}, u32[]{:S(2)}) %all-to-all-start.1) | async-done | bytes 589856 | tf_op jit(solution)/shard_map/all_to_all | solution.py:120
  77.9 16.4 %all-gather.4.cloned.1.call-done = bf16[4096,768]{1,0:T(8,128)(2,1)} async-done(((bf16[128,768]{1,0:T(8,128)(2,1)}), bf16[4096,768]{1,0:T(8,128)(2,1)}) %all-gather.4.cloned.1.call-update) | async-done | bytes 6291472 | tf_op jit(solution)/shard_map/all_gather | solution.py:92
  94.3 33.8 %while.37 = (s32[]{:T(128)}, f32[8,512]{1,0:T(8,128)S(1)}, f32[8,512]{1,0:T(8,128)}, bf16[8,512,768]{2,1,0:T(8,128)(2,1)}, bf16[768,768]{1,0:T(8,128)(2,1)}, /*index=5*/f32[768]{0:T(1024)S(1)}, s32[]{:T(128)}, s32[]{:T(128)}) while((s32[]{:T(128)}, f32[8,512]{1,0:T(8,128)S(1)}, f32[8,512]{1,0:T(8,128)}, bf16[8,512,768]{2,1,0:T(8,128)(2,1)}, ...), condition=%wide.region_4.5_spmd, body=%wide.region_1.4_spmd.sunk | while | flops 605944832 | bytes 5129821 | solution.py:41
  128.7 33.0 %all-gather = f32[32,1,4096]{2,1,0:T(1,128)S(1)} all-gather(f32[1,1,4096]{2,1,0:T(1,128)S(1)} %reshape.145), channel_id=1, replica_groups=mesh['blk'=32,'dp'=8] {'blk'}, dimensions={0}, use_global_device_ids=true | all-gather | bytes 540672 | tf_op jit(solution)/shard_map/all_gather | solution.py:12
  161.8 34.3 %all-gather.1 = f32[32,1,4096]{2,1,0:T(1,128)S(1)} all-gather(f32[1,1,4096]{2,1,0:T(1,128)S(1)} %reshape.147), channel_id=1, replica_groups=mesh['blk'=32,'dp'=8] {'blk'}, dimensions={0}, use_global_device_ids=true | all-gather | bytes 540672 | tf_op jit(solution)/shard_map/all_gather | solution.py:12
  197.5 30.3 %while.38 = (s32[]{:T(128)}, f32[4096]{0:T(1024)S(1)}, f32[4096]{0:T(1024)S(1)}, f32[31,4096]{1,0:T(8,128)}, f32[31,4096]{1,0:T(8,128)S(1)}, /*index=5*/s32[]{:T(128)}) while((s32[]{:T(128)}, f32[4096]{0:T(1024)S(1)}, f32[4096]{0:T(1024)S(1)}, f32[31,4096]{1,0:T(8,128)}, f32[31,4096]{1,0:T(8,128)S(1)}, /*index=5*/s32[]{:T(128)}) %tuple.87), condition=%wide.region_6.7_spmd, body=%wide.region_5.6_spmd.sunk | while | flops 24578 | bytes 163913 | solution.py:15
  227.8 44.6 %while.39 = (s32[]{:T(128)}, f32[768,768]{1,0:T(8,128)S(1)}, f32[768]{0:T(1024)}, bf16[8,512,768]{2,1,0:T(8,128)(2,1)}, bf16[768,768]{1,0:T(8,128)(2,1)}, /*inde...) while((s32[]{:T(128)}, f32[768,768]{1,0:T(8,128)S(1)}, ...), condition=%wide.region_9.10_spmd.clone, body=%wide.region_7.9_spmd.clone.sunk | while | flops 1211892480 | bytes 9098412 | solution.py:65
  227.8 2.4 convert_reduce_fusion.3
  230.3 2.5 select_add_fusion.4
  235.9 2.5 select_add_fusion.4
  241.4 2.5 select_add_fusion.4
  247.0 2.5 select_add_fusion.4
  250.1 2.4 convert_reduce_fusion.3
  252.6 2.5 select_add_fusion.4
  258.2 2.5 select_add_fusion.4
  263.7 2.5 select_add_fusion.4
  269.3 2.5 select_add_fusion.4
  273.9 23.1 %all-reduce = (f32[768]{0:T(1024)S(1)}, f32[64]{0:T(128)S(1)}) all-reduce(f32[768]{0:T(1024)S(1)} %copy-done.3, f32[64]{0:T(128)S(1)} %convert_reduce_fusion.1), channel_id=1, replica_groups=mesh['blk'=32,'dp'=8] {'dp'}, use_global_device_ids=true, to_apply=%region_11.12 | all-reduce | flops 832 | bytes 6656 | tf_op jit(solution)/shard_map/psum | solution.py:143
  297.1 107.2 %all-reduce.4.cloned.1.call-done = (f32[768,768]{1,0:T(8,128)}, f32[64,768]{1,0:T(8,128)}) async-done(((f32[768,768]{1,0:T(8,128)}, f32[64,768]{1,0:T(8,128)}), (f32[768,768]{1,0:T(8,128)}, f32[64,768]{1,0:T(8,128)})) %all-reduce.4.cloned.1.call-update) | async-done | bytes 2555920 | tf_op jit(solution)/shard_map/psum | solution.py:143
  406.0 3.7 fusion.11
  (202 shorter events, 99.8 us)
Async XLA Ops:
  7.2 87.2 %all-gather.4.cloned.1.call-start = ((), (), s32[]{:S(2)}) async-start(), calls=%async_computation.2 | async-start | bytes 6488064 | tf_op jit(solution)/shard_map/all_gather | solution.py:92
  22.6 17.3 %all-to-all-start = ((bf16[32,2,384]{2,1,0:T(2,128)(2,1)}), bf16[32,2,384]{2,1,0:T(2,128)(2,1)S(1)}, u32[]{:S(2)}, u32[]{:S(2)}) async-start(bf16[32,2,384]{2,1,0:T(2,128)(2,1)} %reshape.162), calls=%async_computation | async-start | bytes 98304 | tf_op jit(solution)/shard_map/all_to_all | solution.py:127
  39.9 36.9 %all-to-all-start.1 = ((bf16[32,12,768]{2,1,0:T(8,128)(2,1)}), bf16[32,12,768]{2,1,0:T(8,128)(2,1)S(1)}, u32[]{:S(2)}, u32[]{:S(2)}) async-start(bf16[32,12,768]{2,1,0:T(8,128)(2,1)} %reshape.128), calls=%async_computation.1 | async-start | bytes 1572864 | tf_op jit(solution)/shard_map/all_to_all | solution.py:120
  45.0 359.4 %all-reduce.4.cloned.1.call-start = ((), (), s32[]{:S(2)}) async-start(), calls=%async_computation.3 | async-start | bytes 5111808 | tf_op jit(solution)/shard_map/psum | solution.py:143
  128.1 0.6 copy-start.5
  128.1 33.6 %copy-start.4 = (f32[8,512]{1,0:T(8,128)S(1)}, f32[8,512]{1,0:T(8,128)}, u32[]{:S(2)}) copy-start(f32[8,512]{1,0:T(8,128)} %get-tuple-element.107) | copy-start | bytes 49156
  230.3 2.5 copy-start.1
  232.8 0.6 copy-start.2
  235.9 2.5 copy-start.1
  238.4 0.6 copy-start.2
  241.4 2.5 copy-start.1
  244.0 0.6 copy-start.2
  247.0 2.5 copy-start.1
  249.5 0.6 copy-start.2
  252.6 2.5 copy-start.1
  255.1 0.6 copy-start.2
  258.2 2.5 copy-start.1
  260.7 0.6 copy-start.2
  263.7 2.5 copy-start.1
  266.3 0.6 copy-start.2
  269.3 2.5 copy-start.1
  271.8 0.6 copy-start.2
  272.4 1.4 copy-start
  272.4 1.5 copy-start.3
Sparse Core Ops, SparseCore 0:
  9.9 84.4 all-gather.3
  274.0 130.2 all-reduce.3
where the time goes:
time: 419 us; the launch traced here: 417 us
  waiting for transfers between devices  160 us (38%)
  blocking collectives  90.3 us (22%)
  matrix products  59.7 us (14%)
  local copies, waits for them, and re-layouts  52 us (12%)
  other arithmetic  24.8 us (6%)
  starting transfers between devices  14.5 us (3%)
  between operations  14.3 us (3%)
    psum x1, waiting for transfers between devices, local(): lax.psum((weighted, mass, shift_sum, shift_count), 'dp')  107 us
    all_gather x2, blocking collectives, merged(): pieces = jax.tree.map(lambda part: lax.all_gather(part, axis), value)  67.2 us
    dot_general x16, matrix products, score_block(): lax.dot_general(rows, codebook, (((1,), (1,)), ((), ())), preferred_eleme...  38.8 us
    all_to_all x1, waiting for transfers between devices, local(): lax.all_to_all(row_buffer.reshape(nblk, capacity, width), 'blk', split_ax...  30.1 us
    dynamic_slice x31, local copies, waits for them, and re-layouts, merged(): lax.scan(lambda running, section: (join(running, section), None), head, t...  28.9 us
    psum x1, blocking collectives, local(): lax.psum((weighted, mass, shift_sum, shift_count), 'dp')  23.1 us
    dot_general x8, matrix products, add_weights(): lax.dot_general(weights, block, (((0,), (0,)), ((), ())), preferred_eleme...  19.9 us
    all_gather x1, waiting for transfers between devices, local(): lax.all_gather(residuals, 'blk', axis=0, tiled=True)  16.4 us
  transfers between devices with their start and end apart: 4, of which 4 were waited for; matrix products, arithmetic and copies ran while one was open for 5% of the time, Pallas kernels for 0%

commit v1 on v0

--- a/solution.py
+++ b/solution.py
@@ -89,7 +89,15 @@
     total = total_all
     weighted, mass = accumulate(
         zero_sums,
-        lax.all_gather(residuals, "blk", axis=0, tiled=True),
+        jnp.concatenate(
+            jax.lax.all_to_all(
+                jnp.stack([residuals for _ in range(jax.lax.axis_size("blk"))]),
+                axis_name="blk",
+                split_axis=0,
+                concat_axis=0,
+            ),
+            0,
+        ),
         top,
         total,
         codebook,

time: 419 us -> 510 us (1.22)
  blocking collectives: 90.3 us -> 164 us
  waiting for transfers between devices: 160 us -> 169 us
    all_gather x2, blocking collectives: 67.2 us -> 140 us  [merged(): pieces = jax.tree.map(lambda part: lax.all_gather(part, axis), value)]
    all_gather x1, waiting for transfers between devices: 16.4 us -> 25.1 us  [local(): lax.all_gather(residuals, 'blk', axis=0, tiled=True)]
  transfers between devices with their start and end apart: 4 -> 5, of which waited for: 4 -> 4; matrix products, arithmetic and copies ran while one was open for 5% -> 18% of each run, Pallas kernels for 0% -> 0%
where the time goes in v1:
time: 510 us; the launch traced here: 508 us
  waiting for transfers between devices  169 us (33%)
  blocking collectives  164 us (32%)
  matrix products  59.7 us (12%)
  local copies, waits for them, and re-layouts  56.2 us (11%)
  other arithmetic  24.8 us (5%)
  starting transfers between devices  19.2 us (4%)
  between operations  14.3 us (3%)
    all_gather x2, blocking collectives, merged(): pieces = jax.tree.map(lambda part: lax.all_gather(part, axis), value)  140 us
    psum x1, waiting for transfers between devices, local(): lax.psum((weighted, mass, shift_sum, shift_count), 'dp')  108 us
    dot_general x16, matrix products, score_block(): lax.dot_general(rows, codebook, (((1,), (1,)), ((), ())), preferred_eleme...  38.8 us
    all_to_all x1, waiting for transfers between devices, local(): lax.all_to_all(row_buffer.reshape(nblk, capacity, width), 'blk', split_ax...  30.2 us
    dynamic_slice x31, local copies, waits for them, and re-layouts, merged(): lax.scan(lambda running, section: (join(running, section), None), head, t...  28.9 us
    all_gather x1, waiting for transfers between devices, local(): lax.all_gather(residuals, 'blk', axis=0, tiled=True)  25.1 us
    psum x1, blocking collectives, local(): lax.psum((weighted, mass, shift_sum, shift_count), 'dp')  23.3 us
    dot_general x8, matrix products, add_weights(): lax.dot_general(weights, block, (((0,), (0,)), ((), ())), preferred_eleme...  19.9 us
  transfers between devices with their start and end apart: 5, of which 4 were waited for; matrix products, arithmetic and copies ran while one was open for 18% of the time, Pallas kernels for 0%

profile of v1, /device:TPU:50, one launch (start us, length us, event | category | flops | bytes accessed | tf_op | source)
XLA Modules:
  0.0 508.0 jit_solution(12497724867154783689)
XLA Ops:
  8.6 9.0 %reduce-window.6 = s32[32,8,128]{2,1,0:T(8,128)S(1)} reduce-window(s32[32,8,128]{2,1,0:T(8,128)S(1)} %fusion.18, s32[]{:T(128)} %constant.71.clone.1), window={size=1x1x128 pad=0_0x0_0x127_0}, to_apply=%region_12.13 | reduce-window | flops 4161536 | bytes 262148 | tf_op jit(solution)/shard_map/reduce-window
  22.6 9.4 %all-to-all-start.1 = ((bf16[32,2,384]{2,1,0:T(2,128)(2,1)}), bf16[32,2,384]{2,1,0:T(2,128)(2,1)S(1)}, u32[]{:S(2)}, u32[]{:S(2)}) async-start(bf16[32,2,384]{2,1,0:T(2,128)(2,1)} %reshape.163), calls=%async_computation.1 | async-start | bytes 98304 | tf_op jit(solution)/shard_map/all_to_all | solution.py:135
  34.9 5.1 %all-to-all-done.1 = bf16[32,2,384]{2,1,0:T(2,128)(2,1)S(1)} async-done(((bf16[32,2,384]{2,1,0:T(2,128)(2,1)}), bf16[32,2,384]{2,1,0:T(2,128)(2,1)S(1)}, u32[]{:S(2)}, u32[]{:S(2)}) %all-to-all-start.1) | async-done | bytes 49184 | tf_op jit(solution)/shard_map/all_to_all | solution.py:135
  39.9 5.0 all-to-all-start.2
  46.7 30.2 %all-to-all-done.2 = bf16[32,12,768]{2,1,0:T(8,128)(2,1)S(1)} async-done(((bf16[32,12,768]{2,1,0:T(8,128)(2,1)}), bf16[32,12,768]{2,1,0:T(8,128)(2,1)S(1)}, u32[]{:S(2)}, u32[]{:S(2)}) %all-to-all-start.2) | async-done | bytes 589856 | tf_op jit(solution)/shard_map/all_to_all | solution.py:128
  76.9 3.4 stack.2
  80.2 4.7 all-to-all-start
  86.0 25.1 %all-gather.4.cloned.1.call-done = bf16[4096,768]{1,0:T(8,128)(2,1)} async-done(((bf16[128,768]{1,0:T(8,128)(2,1)}), bf16[4096,768]{1,0:T(8,128)(2,1)}) %all-gather.4.cloned.1.call-update) | async-done | bytes 6291472 | tf_op jit(solution)/shard_map/all_gather | solution.py:80
  111.2 33.8 %while.37 = (s32[]{:T(128)}, f32[8,512]{1,0:T(8,128)S(1)}, f32[8,512]{1,0:T(8,128)}, bf16[8,512,768]{2,1,0:T(8,128)(2,1)}, bf16[768,768]{1,0:T(8,128)(2,1)}, /*index=5*/f32[768]{0:T(1024)S(1)}, s32[]{:T(128)}, s32[]{:T(128)}) while((s32[]{:T(128)}, f32[8,512]{1,0:T(8,128)S(1)}, f32[8,512]{1,0:T(8,128)}, bf16[8,512,768]{2,1,0:T(8,128)(2,1)}, ...), condition=%wide.region_4.5_spmd, body=%wide.region_1.4_spmd.sunk | while | flops 605944832 | bytes 5129821 | solution.py:41
  145.6 104.2 %all-gather = f32[32,1,4096]{2,1,0:T(1,128)S(1)} all-gather(f32[1,1,4096]{2,1,0:T(1,128)S(1)} %reshape.146), channel_id=1, replica_groups=mesh['blk'=32,'dp'=8] {'blk'}, dimensions={0}, use_global_device_ids=true | all-gather | bytes 540672 | tf_op jit(solution)/shard_map/all_gather | solution.py:12
  250.6 36.3 %all-gather.1 = f32[32,1,4096]{2,1,0:T(1,128)S(1)} all-gather(f32[1,1,4096]{2,1,0:T(1,128)S(1)} %reshape.148), channel_id=1, replica_groups=mesh['blk'=32,'dp'=8] {'blk'}, dimensions={0}, use_global_device_ids=true | all-gather | bytes 540672 | tf_op jit(solution)/shard_map/all_gather | solution.py:12
  288.3 30.3 %while.38 = (s32[]{:T(128)}, f32[4096]{0:T(1024)S(1)}, f32[4096]{0:T(1024)S(1)}, f32[31,4096]{1,0:T(8,128)}, f32[31,4096]{1,0:T(8,128)S(1)}, /*index=5*/s32[]{:T(128)}) while((s32[]{:T(128)}, f32[4096]{0:T(1024)S(1)}, f32[4096]{0:T(1024)S(1)}, f32[31,4096]{1,0:T(8,128)}, f32[31,4096]{1,0:T(8,128)S(1)}, /*index=5*/s32[]{:T(128)}) %tuple.85), condition=%wide.region_6.7_spmd, body=%wide.region_5.6_spmd.sunk | while | flops 24578 | bytes 163913 | solution.py:15
  318.6 44.7 %while.39 = (s32[]{:T(128)}, f32[768,768]{1,0:T(8,128)S(1)}, f32[768]{0:T(1024)}, bf16[8,512,768]{2,1,0:T(8,128)(2,1)}, bf16[768,768]{1,0:T(8,128)(2,1)}, /*inde...) while((s32[]{:T(128)}, f32[768,768]{1,0:T(8,128)S(1)}, ...), condition=%wide.region_9.10_spmd.clone, body=%wide.region_7.9_spmd.clone.sunk | while | flops 1211892480 | bytes 9098412 | solution.py:65
  321.1 2.5 select_add_fusion.4
  326.7 2.5 select_add_fusion.4
  332.3 2.5 select_add_fusion.4
  337.9 2.5 select_add_fusion.4
  343.5 2.5 select_add_fusion.4
  349.0 2.5 select_add_fusion.4
  354.6 2.5 select_add_fusion.4
  360.2 2.5 select_add_fusion.4
  364.8 23.3 %all-reduce = (f32[768]{0:T(1024)S(1)}, f32[64]{0:T(128)S(1)}) all-reduce(f32[768]{0:T(1024)S(1)} %copy-done.4, f32[64]{0:T(128)S(1)} %convert_reduce_fusion.1), channel_id=1, replica_groups=mesh['blk'=32,'dp'=8] {'dp'}, use_global_device_ids=true, to_apply=%region_11.12 | all-reduce | flops 832 | bytes 6656 | tf_op jit(solution)/shard_map/psum | solution.py:151
  388.1 107.6 %all-reduce.4.cloned.1.call-done = (f32[768,768]{1,0:T(8,128)}, f32[64,768]{1,0:T(8,128)}) async-done(((f32[768,768]{1,0:T(8,128)}, f32[64,768]{1,0:T(8,128)}), (f32[768,768]{1,0:T(8,128)}, f32[64,768]{1,0:T(8,128)})) %all-reduce.4.cloned.1.call-update) | async-done | bytes 2555920 | tf_op jit(solution)/shard_map/psum | solution.py:151
  497.4 3.7 fusion.11
  (205 shorter events, 105.5 us)
Async XLA Ops:
  7.2 104.0 %all-gather.4.cloned.1.call-start = ((), (), s32[]{:S(2)}) async-start(), calls=%async_computation.3 | async-start | bytes 6488064 | tf_op jit(solution)/shard_map/all_gather | solution.py:80
  22.6 17.3 %all-to-all-start.1 = ((bf16[32,2,384]{2,1,0:T(2,128)(2,1)}), bf16[32,2,384]{2,1,0:T(2,128)(2,1)S(1)}, u32[]{:S(2)}, u32[]{:S(2)}) async-start(bf16[32,2,384]{2,1,0:T(2,128)(2,1)} %reshape.163), calls=%async_computation.1 | async-start | bytes 98304 | tf_op jit(solution)/shard_map/all_to_all | solution.py:135
  32.1 44.8 %copy-start.1 = (bf16[128,768]{1,0:T(8,128)(2,1)S(1)}, bf16[128,768]{1,0:T(8,128)(2,1)}, u32[]{:S(2)}) copy-start(bf16[128,768]{1,0:T(8,128)(2,1)} %param.10) | copy-start | bytes 589828
  39.9 36.9 %all-to-all-start.2 = ((bf16[32,12,768]{2,1,0:T(8,128)(2,1)}), bf16[32,12,768]{2,1,0:T(8,128)(2,1)S(1)}, u32[]{:S(2)}, u32[]{:S(2)}) async-start(bf16[32,12,768]{2,1,0:T(8,128)(2,1)} %reshape.129), calls=%async_computation.2 | async-start | bytes 1572864 | tf_op jit(solution)/shard_map/all_to_all | solution.py:128
  80.2 238.4 %all-to-all-start = ((bf16[32,128,768]{2,1,0:T(8,128)(2,1)}), bf16[32,128,768]{2,1,0:T(8,128)(2,1)}, u32[]{:S(2)}, u32[]{:S(2)}) async-start(bf16[32,128,768]{2,1,0:T(8,128)(2,1)} %stack.2), calls=%async_computation | async-start | bytes 12582912 | tf_op jit(solution)/shard_map/all_to_all | solution.py:93
  85.0 410.8 %all-reduce.4.cloned.1.call-start = ((), (), s32[]{:S(2)}) async-start(), calls=%async_computation.4 | async-start | bytes 5111808 | tf_op jit(solution)/shard_map/psum | solution.py:151
  321.1 2.5 copy-start.2
  323.6 0.6 copy-start.3
  326.7 2.5 copy-start.2
  329.2 0.6 copy-start.3
  332.3 2.5 copy-start.2
  334.8 0.6 copy-start.3
  337.9 2.5 copy-start.2
  340.4 0.6 copy-start.3
  343.5 2.5 copy-start.2
  346.0 0.6 copy-start.3
  349.0 2.5 copy-start.2
  351.6 0.6 copy-start.3
  354.6 2.5 copy-start.2
  357.1 0.6 copy-start.3
  360.2 2.5 copy-start.2
  362.7 0.6 copy-start.3
  363.3 1.4 copy-start
  363.3 1.5 copy-start.4
  (1 other events, 0.6 us)
Sparse Core Ops, SparseCore 0:
  9.9 101.2 all-gather.3
  364.9 130.8 all-reduce.3
